TPU v7x, 32 devices: a whole 2x2x4 slice. The times are simulated.
32 devices in a mesh: dev: 32 (over z, y, x, core).
Axes of the slice: x: 2, y: 2, z: 4, core: 2. Of those that a mesh axis runs over, the one named last changes fastest.
Arguments:
- planes: bfloat16 [128, 19, 19, 17], P('dev'), may hold values from 0 to 1, as said below
- history: int32 [128, 8], P('dev'), may hold values from 0 to 1, as said below
- stem_kernel: bfloat16 [39168], P('dev'), may hold values from -0.5 to 0.5
- stem_gain: bfloat16 [256], P('dev'), may hold values from 0.5 to 1.5
- stem_shift: bfloat16 [256], P('dev'), may hold values from -3 to 3
- first_kernel: bfloat16 [589824], P('dev'), may hold values from -0.125 to 0.125
- first_gain: bfloat16 [256], P('dev'), may hold values from 0.5 to 1.5
- first_shift: bfloat16 [256], P('dev'), may hold values from -3 to 3
- second_kernel: bfloat16 [589824], P('dev'), may hold values from -0.125 to 0.125
- second_gain: bfloat16 [256], P('dev'), may hold values from 0.5 to 1.5
- second_shift: bfloat16 [256], P('dev'), may hold values from -3 to 3
- cotangent: bfloat16 [128, 19, 19, 256], P('dev'), may hold values from -6 to 6
Outputs:
- activations: bfloat16 [128, 19, 19, 256], P('dev')
- planes_grad: float32 [128, 19, 19, 17], P('dev')
- stem_kernel_grad: float32 [39168], P('dev')
- stem_gain_grad: float32 [256], P('dev')
- stem_shift_grad: float32 [256], P('dev')
- first_kernel_grad: float32 [589824], P('dev')
- first_gain_grad: float32 [256], P('dev')
- first_shift_grad: float32 [256], P('dev')
- second_kernel_grad: float32 [589824], P('dev')
- second_gain_grad: float32 [256], P('dev')
- second_shift_grad: float32 [256], P('dev')
Inputs may be any that keep to these rules, and one draw needn't show every extreme that they name: `planes`: each entry is 0 or 1; the last plane is constant over a position's squares. The available history slots of a position are its first ones; the first slot is always available.
All inputs are finite; a program needn't handle non-finite values.
Results may differ from a plain program's by a relative error of at most 0.0075.
Values may be sent and summed in bfloat16 or wider, within the bound.
A program may use at most 128 MiB of HBM per device.

v0:
```python
import jax
import jax.numpy as jnp
from jax import lax
from jax.sharding import PartitionSpec as P

epsilon = 1e-05


def swish(value):
    return value * jax.nn.sigmoid(value)


def swish_slope(value):
    sigma = jax.nn.sigmoid(value)
    return sigma * (1.0 + value * (1.0 - sigma))


def project(source, kernel_all):
    return lax.conv_general_dilated(
        source,
        kernel_all,
        (1, 1),
        "SAME",
        dimension_numbers=("NHWC", "HWIO", "NHWC"),
        preferred_element_type=jnp.float32,
    )


def transpose_conv(gradient, kernel_all):
    flipped = jnp.transpose(kernel_all[::-1, ::-1], (0, 1, 3, 2))
    return project(gradient, flipped)


def kernel_product(source, gradient):
    return lax.conv_general_dilated(
        source,
        gradient,
        (1, 1),
        ((1, 1), (1, 1)),
        dimension_numbers=("CHWN", "IHWO", "HWNC"),
        preferred_element_type=jnp.float32,
    )


def gather_layer(kernel, gain, shift, channels_in):
    kernel_all, gain_all, shift_all = (
        lax.all_gather(kernel, "dev", axis=0, tiled=True),
        lax.all_gather(gain, "dev", axis=0, tiled=True),
        lax.all_gather(shift, "dev", axis=0, tiled=True),
    )
    return (
        kernel_all.reshape(3, 3, channels_in, -1),
        gain_all.astype(jnp.float32),
        shift_all.astype(jnp.float32),
    )


def statistics(pre_value):
    total_cells = (
        pre_value.shape[0] * pre_value.shape[1] * pre_value.shape[2] * lax.axis_size("dev")
    )
    centre = lax.psum(jnp.sum(pre_value, axis=(0, 1, 2)), "dev") / total_cells
    deviation = pre_value - centre
    variance = lax.psum(jnp.sum(deviation * deviation, axis=(0, 1, 2)), "dev") / total_cells
    return (centre, lax.rsqrt(variance + epsilon))


def normalize(pre_value, stats, weights):
    normed = (pre_value - stats[0]) * stats[1]
    return (normed, normed * weights[1] + weights[2])


def share_kernel(kernel_grad):
    return lax.psum_scatter(kernel_grad.reshape(-1), "dev", scatter_dimension=0, tiled=True)


def layer_back(source, weights, stats, normed, norm_grad):
    kernel_all, gain_all, shift_all = weights
    total_cells = (
        norm_grad.shape[0] * norm_grad.shape[1] * norm_grad.shape[2] * lax.axis_size("dev")
    )
    shift_grad, gain_grad = lax.psum(
        (jnp.sum(norm_grad, axis=(0, 1, 2)), jnp.sum(norm_grad * normed, axis=(0, 1, 2))), "dev"
    )
    pre_grad = (
        gain_all
        * stats[1]
        * (norm_grad - shift_grad / total_cells - normed * gain_grad / total_cells)
    ).astype(jnp.bfloat16)
    kernel_shard = share_kernel(kernel_product(source, pre_grad))
    source_grad = transpose_conv(pre_grad, kernel_all)
    shard_len = gain_all.shape[0] // lax.axis_size("dev")
    start = lax.axis_index("dev") * shard_len
    return (
        source_grad,
        kernel_shard,
        lax.dynamic_slice_in_dim(gain_grad, start, shard_len),
        lax.dynamic_slice_in_dim(shift_grad, start, shard_len),
    )


def body(
    planes,
    history,
    stem_kernel,
    stem_gain,
    stem_shift,
    first_kernel,
    first_gain,
    first_shift,
    second_kernel,
    second_gain,
    second_shift,
    cotangent,
):
    plane_count = planes.shape[3]
    present = jnp.concatenate(
        [jnp.repeat(history, 2, axis=1), jnp.ones((history.shape[0], 1), jnp.int32)], axis=1
    ).astype(jnp.float32)[:, None, None, :]
    stem_input = (planes.astype(jnp.float32) * present).astype(jnp.bfloat16)
    stem_weights = gather_layer(stem_kernel, stem_gain, stem_shift, plane_count)
    channels = stem_weights[1].shape[0]
    stem_pre = project(stem_input, stem_weights[0])
    stem_stats = statistics(stem_pre)
    stem_normed, stem_norm = normalize(stem_pre, stem_stats, stem_weights)
    stem_act = swish(stem_norm).astype(jnp.bfloat16)
    first_weights = gather_layer(first_kernel, first_gain, first_shift, channels)
    first_pre = project(stem_act, first_weights[0])
    first_stats = statistics(first_pre)
    first_normed, first_norm = normalize(first_pre, first_stats, first_weights)
    first_act = swish(first_norm).astype(jnp.bfloat16)
    second_weights = gather_layer(second_kernel, second_gain, second_shift, channels)
    second_pre = project(first_act, second_weights[0])
    second_stats = statistics(second_pre)
    second_normed, second_norm = normalize(second_pre, second_stats, second_weights)
    summed = second_norm + stem_act.astype(jnp.float32)
    activations = swish(summed).astype(jnp.bfloat16)
    second_back = gather_layer(second_kernel, second_gain, second_shift, channels)
    second_normed, second_norm = normalize(
        project(first_act, second_back[0]), second_stats, second_back
    )
    summed_grad = cotangent.astype(jnp.float32) * swish_slope(
        second_norm + stem_act.astype(jnp.float32)
    )
    first_act_grad, second_kernel_grad, second_gain_grad, second_shift_grad = layer_back(
        first_act, second_back, second_stats, second_normed, summed_grad
    )
    first_back = gather_layer(first_kernel, first_gain, first_shift, channels)
    first_normed, first_norm = normalize(project(stem_act, first_back[0]), first_stats, first_back)
    stem_conv_grad, first_kernel_grad, first_gain_grad, first_shift_grad = layer_back(
        stem_act, first_back, first_stats, first_normed, first_act_grad * swish_slope(first_norm)
    )
    stem_back = gather_layer(stem_kernel, stem_gain, stem_shift, plane_count)
    stem_normed, stem_norm = normalize(project(stem_input, stem_back[0]), stem_stats, stem_back)
    input_grad, stem_kernel_grad, stem_gain_grad, stem_shift_grad = layer_back(
        stem_input,
        stem_back,
        stem_stats,
        stem_normed,
        (stem_conv_grad + summed_grad) * swish_slope(stem_norm),
    )
    planes_grad = input_grad * present
    return (
        activations,
        planes_grad,
        stem_kernel_grad,
        stem_gain_grad,
        stem_shift_grad,
        first_kernel_grad,
        first_gain_grad,
        first_shift_grad,
        second_kernel_grad,
        second_gain_grad,
        second_shift_grad,
    )


def solution(mesh):
    return jax.shard_map(
        body,
        mesh=mesh,
        in_specs=(
            P("dev", None, None, None),
            P("dev", None),
            P("dev"),
            P("dev"),
            P("dev"),
            P("dev"),
            P("dev"),
            P("dev"),
            P("dev"),
            P("dev"),
            P("dev"),
            P("dev", None, None, None),
        ),
        out_specs=(
            P("dev", None, None, None),
            P("dev", None, None, None),
            P("dev"),
            P("dev"),
            P("dev"),
            P("dev"),
            P("dev"),
            P("dev"),
            P("dev"),
            P("dev"),
            P("dev"),
        ),
        check_vma=False,
    )
```

profile of v0, /device:TPU:0, one launch (start us, length us, event | category | flops | bytes accessed | tf_op | source)
XLA Modules:
  0.0 791.2 jit_solution(1301726509166178640)
XLA Ops:
  11.1 1.2 fusion.88
  12.3 1.2 multiply_convert_fusion.4
  17.2 42.1 %all-reduce.15 = (bf16[256]{0:T(256)(128)(2,1)S(1)}, bf16[256]{0:T(256)(128)(2,1)S(1)}, bf16[256]{0:T(256)(128)(2,1)S(1)}, bf16[256]{0:T(256)(128)(2,1)S(1)}, bf...) all-reduce(bf16[256]{0:T(256)(128)(2,1)S(1)} %dynamic-update-slice.2, ...), channel_id=1, replica_groups=mesh['dev'=32] {'dev'}, use_global_device_ids=true, to_apply=%add.3 | all-reduce | flops 1536 | bytes 6144
  59.4 1.4 copy.138
  60.7 75.5 %all-reduce.19.cloned.1.call-done = bf16[39168]{0:T(1024)(128)(2,1)} async-done(((bf16[39168]{0:T(1024)(128)(2,1)}), bf16[39168]{0:T(1024)(128)(2,1)}) %all-reduce.19.cloned.1.call-update) | async-done | bytes 78352
  136.2 0.9 reshape.69
  137.1 1.1 select_reduce_fusion.7
  138.2 42.4 %psum.84 = f32[256]{0:T(256)S(1)} all-reduce(f32[256]{0:T(256)S(1)} %get-tuple-element.102), channel_id=1, replica_groups=mesh['dev'=32] {'dev'}, use_global_device_ids=true, to_apply=%region_1.0 | all-reduce | flops 256 | bytes 2048 | tf_op jit(solution)/shard_map/psum | solution.py:62
  181.1 40.2 %psum.85 = f32[256]{0:T(256)S(1)} all-reduce(f32[256]{0:T(256)S(1)} %select_reduce_fusion.6), channel_id=1, replica_groups=mesh['dev'=32] {'dev'}, use_global_device_ids=true, to_apply=%region_3.0 | all-reduce | flops 256 | bytes 2048 | tf_op jit(solution)/shard_map/psum | solution.py:64
  221.8 1.8 fusion.57
  225.2 2.8 copy.131
  228.0 4.2 reshape.149
  232.3 1.4 maximum_bitcast_fusion.4
  233.7 3.0 reshape.70
  236.7 4.1 select_reduce_fusion.5
  240.8 40.2 %psum.86 = f32[256]{0:T(256)S(1)} all-reduce(f32[256]{0:T(256)S(1)} %get-tuple-element.104), channel_id=1, replica_groups=mesh['dev'=32] {'dev'}, use_global_device_ids=true, to_apply=%region_5.0 | all-reduce | flops 256 | bytes 2048 | tf_op jit(solution)/shard_map/psum | solution.py:62
  281.3 40.1 %psum.87 = f32[256]{0:T(256)S(1)} all-reduce(f32[256]{0:T(256)S(1)} %select_reduce_fusion.4), channel_id=1, replica_groups=mesh['dev'=32] {'dev'}, use_global_device_ids=true, to_apply=%region_7.0 | all-reduce | flops 256 | bytes 2048 | tf_op jit(solution)/shard_map/psum | solution.py:64
  322.9 1.3 fusion.73
  324.2 1.6 fusion.86
  325.8 3.0 reshape.71
  328.8 5.2 select_reduce_fusion.3
  334.0 40.3 %psum.88 = f32[256]{0:T(256)S(1)} all-reduce(f32[256]{0:T(256)S(1)} %get-tuple-element.106), channel_id=1, replica_groups=mesh['dev'=32] {'dev'}, use_global_device_ids=true, to_apply=%region_9.0 | all-reduce | flops 256 | bytes 2048 | tf_op jit(solution)/shard_map/psum | solution.py:62
  374.3 1.9 select_reduce_fusion.2
  376.2 40.2 %psum.89 = f32[256]{0:T(256)S(1)} all-reduce(f32[256]{0:T(256)S(1)} %select_reduce_fusion.2), channel_id=1, replica_groups=mesh['dev'=32] {'dev'}, use_global_device_ids=true, to_apply=%region_11.0 | all-reduce | flops 256 | bytes 2048 | tf_op jit(solution)/shard_map/psum | solution.py:64
  416.9 5.3 add_multiply_fusion
  422.3 2.8 copy.124
  425.0 4.2 reshape.139
  429.2 4.3 copy.125
  433.5 4.2 reshape.141
  437.7 3.1 fusion.70
  440.8 40.6 %all-reduce.13 = (f32[256]{0:T(256)}, f32[256]{0:T(256)}) all-reduce(f32[256]{0:T(256)} %get-tuple-element.56, f32[256]{0:T(256)} %get-tuple-element.55), channel_id=1, replica_groups=mesh['dev'=32] {'dev'}, use_global_device_ids=true, to_apply=%region_15.0 | all-reduce | flops 512 | bytes 4096 | tf_op jit(solution)/shard_map/psum | solution.py:82
  481.4 3.2 multiply_multiply_fusion
  484.6 2.8 copy.126
  487.4 4.2 reshape.143
  491.5 2.6 fusion.53
  494.1 1.2 copy.148
  495.4 1.4 reshape.112
  496.9 1.8 maximum_bitcast_fusion.6
  499.0 2.8 fusion.4
  501.8 2.6 copy.151
  506.2 4.6 select_reduce_fusion
  510.8 40.1 %all-reduce.12 = (f32[256]{0:T(256)S(1)}, f32[256]{0:T(256)}) all-reduce(f32[256]{0:T(256)S(1)} %get-tuple-element.58, f32[256]{0:T(256)S(1)} %get-tuple-element.57), channel_id=1, replica_groups=mesh['dev'=32] {'dev'}, use_global_device_ids=true, to_apply=%region_17.0 | all-reduce | flops 512 | bytes 4096 | tf_op jit(solution)/shard_map/psum | solution.py:82
  551.4 3.0 select_bitcast_fusion
  556.8 4.4 fusion.6
  561.2 2.7 copy.150
  564.0 2.5 fusion.23
  566.5 1.3 copy.129
  567.8 2.2 reshape.145
  570.0 4.3 copy.130
  574.2 4.3 reshape.147
  578.6 4.7 fusion.71
  583.3 40.5 %all-reduce.11 = (f32[256]{0:T(256)S(1)}, f32[256]{0:T(256)S(1)}) all-reduce(f32[256]{0:T(256)S(1)} %get-tuple-element.60, f32[256]{0:T(256)S(1)} %get-tuple-element.59), channel_id=1, replica_groups=mesh['dev'=32] {'dev'}, use_global_device_ids=true, to_apply=%region_23.0 | all-reduce | flops 512 | bytes 4096 | tf_op jit(solution)/shard_map/psum | solution.py:82
  623.8 1.7 multiply_multiply_fusion.1
  625.5 1.3 copy.132
  626.8 2.0 reshape.151
  628.8 2.5 fusion.10
  631.3 1.3 fusion.60
  639.7 5.4 fusion.44
  646.2 1.3 copy.146
  649.3 1.2 copy.145
  650.4 129.4 %all-reduce.21.cloned.1.call-done = (f32[39168]{0:T(1024)}, f32[589824]{0:T(1024)}, f32[589824]{0:T(1024)}) async-done(((f32[39168]{0:T(1024)}, f32[589824]{0:T(1024)}, f32[589824]{0:T(1024)}), (f32[39168]{0:T(1024)}, f32[589824]{0:T(1024)}, f32[589824]{0:T(1024)})) %all-reduce.21.cloned.1.call-update) | async-done | bytes 4875280
  779.8 1.5 dynamic-slice.1
  781.4 1.5 dynamic-slice.2
  782.9 1.4 dynamic-slice
  (181 shorter events, 27.5 us)
Async XLA Ops:
  7.2 129.0 %all-reduce.19.cloned.1.call-start = ((), (), s32[]{:S(2)}) async-start(), calls=%async_computation.2 | async-start | bytes 159744
  8.1 0.6 copy-start.17
  8.8 224.9 %all-gather.3.cloned.1.call-start = ((), (), s32[]{:S(2)}) async-start(), calls=%async_computation | async-start | bytes 1216512 | tf_op jit(solution)/shard_map/all_gather | solution.py:47
  9.6 316.2 %all-gather.5.cloned.1.call-start = ((), (), s32[]{:S(2)}) async-start(), calls=%async_computation.1 | async-start | bytes 1216512 | tf_op jit(solution)/shard_map/all_gather | solution.py:47
  10.3 769.5 %all-reduce.21.cloned.1.call-start = ((), (), s32[]{:S(2)}) async-start(), calls=%async_computation.3 | async-start | bytes 9756672
  14.3 1.4 copy-start.40
  14.3 1.6 copy-start.41
  14.3 1.9 copy-start.42
  14.3 2.1 copy-start.43
  14.4 2.4 copy-start.44
  14.4 2.6 copy-start.45
  14.7 122.4 %copy-start.18 = (pred[32,3]{0,1:T(4,128)(4,1)S(1)}, pred[32,3]{0,1:T(4,128)(4,1)}, u32[]{:S(2)}) copy-start(pred[32,3]{0,1:T(4,128)(4,1)} %constant.84) | copy-start | bytes 292
  59.3 264.9 %copy-start.25 = (f32[256]{0:T(256)}, f32[256]{0:T(256)S(1)}, u32[]{:S(2)}) copy-start(f32[256]{0:T(256)S(1)} %convert_element_type.64) | copy-start | bytes 3076
  59.3 264.9 %copy-start.27 = (f32[256]{0:T(256)}, f32[256]{0:T(256)S(1)}, u32[]{:S(2)}) copy-start(f32[256]{0:T(256)S(1)} %convert_element_type.65) | copy-start | bytes 3076
  59.3 357.6 %copy-start.31 = (f32[256]{0:T(256)}, f32[256]{0:T(256)S(1)}, u32[]{:S(2)}) copy-start(f32[256]{0:T(256)S(1)} %convert_element_type.67) | copy-start | bytes 3076
  59.4 357.6 %copy-start.32 = (f32[256]{0:T(256)}, f32[256]{0:T(256)S(1)}, u32[]{:S(2)}) copy-start(f32[256]{0:T(256)S(1)} %convert_element_type.68) | copy-start | bytes 3076
  137.1 43.9 %copy-start.14 = (bf16[3,3,17,256]{3,2,1,0:T(8,128)(2,1)}, bf16[3,3,17,256]{3,2,1,0:T(8,128)(2,1)S(1)}, u32[]{:S(2)}) copy-start(bf16[3,3,17,256]{3,2,1,0:T(8,128)(2,1)S(1)} %reshape.69) | copy-start | bytes 235012
  223.6 1.6 copy-start.1
  223.7 1.1 copy-start.3
  280.9 43.2 %copy-start.21 = (f32[256]{0:T(256)}, f32[256]{0:T(256)S(1)}, u32[]{:S(2)}) copy-start(f32[256]{0:T(256)S(1)} %broadcast_multiply_fusion.4) | copy-start | bytes 3076
  321.9 2.2 copy-start.23
  322.6 1.6 copy-start.2
  322.8 6.0 copy-start.8
  322.9 5.9 copy-start.9
  433.5 4.3 copy-start.4
  487.3 4.2 copy-start.33
  487.3 4.2 copy-start.29
  496.9 1.9 copy-start.10
  496.9 2.1 copy-start.13
  501.8 2.6 copy-start.6
  504.9 1.3 copy-start.12
  504.9 1.3 copy-start.19
  504.9 1.3 copy-start.22
  504.9 1.2 copy-start.24
  505.0 1.2 copy-start.26
  505.0 1.2 copy-start.28
  550.9 0.6 copy-start.35
  555.3 0.8 copy-start.39
  561.2 2.7 copy-start.7
  561.2 2.8 copy-start.11
  574.2 4.3 copy-start
  626.8 2.0 copy-start.30
  628.8 2.5 copy-start.16
  633.5 2.0 copy-start.38
  633.5 2.6 copy-start.36
  633.5 3.1 copy-start.37
  633.5 3.7 copy-start.34
  638.6 1.1 copy-start.15
  639.7 5.4 copy-start.20
  646.1 1.4 copy-start.5
Sparse Core Ops, SparseCore 0:
  14.2 121.9 all-reduce.18
  139.1 56.0 all-gather.2
  198.0 53.0 all-gather.4
  633.5 146.3 all-reduce.20
where the time goes:
time: 799 us; the launch traced here: 791 us
  blocking collectives  407 us (51%)
  waiting for transfers between devices  206 us (26%)
  local copies, waits for them, and re-layouts  89.2 us (11%)
  other arithmetic  42.7 us (5%)
  matrix products  31.4 us (4%)
  between operations  15 us (2%)
    unnamed x6, waiting for transfers between devices  206 us
    psum x3, blocking collectives, statistics(): centre = lax.psum(jnp.sum(pre_value, axis=(0, 1, 2)), 'dev') / total_cells  123 us
    psum x3, blocking collectives, layer_back(): lax.psum((jnp.sum(norm_grad, axis=(0, 1, 2)), jnp.sum(norm_grad * normed,...  121 us
    psum x3, blocking collectives, statistics(): lax.psum(jnp.sum(deviation * deviation, axis=(0, 1, 2)), 'dev')  120 us
    unnamed x1, blocking collectives  42.1 us
    conv_general_dilated x6, matrix products, project(): lax.conv_general_dilated(source, kernel_all, (1, 1), 'SAME', dimension_nu...  22.8 us
    unnamed x117, local copies, waits for them, and re-layouts  20.4 us
  transfers between devices with their start and end apart: 4, of which 2 were waited for; matrix products, arithmetic and copies ran while one was open for 6% of the time, Pallas kernels for 0%

commit v1 on v0

v1 whole, which is shorter than its diff:
```python
import functools
import math

import jax
import jax.numpy as jnp
from jax import lax
from jax.experimental import pallas as pl
from jax.experimental.pallas import tpu as pltpu
from jax.sharding import PartitionSpec as P

F32 = jnp.float32
BF16 = jnp.bfloat16
MESH = pl.DeviceIdType.MESH
EPSILON = 1e-5
GROUP = 8
QUAD = GROUP // 2


def up(value, step):
    return -(-value // step) * step


class Sizes:
    def __init__(self, n, planes_t, cot_t, stem_len, kernel_len):
        self.n = n
        self.outer = n // GROUP
        self.board, self.planes, self.pos, _ = planes_t
        self.channels = cot_t[3]
        self.block = (self.board + 1) * self.pos
        self.live = self.board * self.pos
        self.rows = self.board * self.block
        self.deep = up(self.rows, 128)
        self.tall = 2 * self.block + self.deep
        self.taps = 9
        self.width = 256
        self.stem_len = stem_len
        self.stem_apart = 2 * stem_len >= 7 * self.channels
        self.stem_all = up(n * stem_len // self.channels, 8) + 8
        self.krows = kernel_len // self.channels
        self.kmsg = up(2 * self.krows + 4, 16)
        self.gmsg = up(2 * self.krows, 16)
        self.vec = self.channels // n
        self.first_row = up(2 * self.krows, 8)
        self.stem_row = 2 * self.first_row
        self.vec_row = self.stem_row + 16
        self.packed = self.vec_row + 8
        self.cells = n * self.pos * self.board * self.board


def iota(shape, axis):
    return lax.broadcasted_iota(jnp.int32, shape, axis)


def wait_bytes(ref, sem):
    pltpu.make_async_copy(ref, ref, sem).wait()


def dot(a, b):
    return lax.dot_general(a, b, (((1,), (0,)), ((), ())), preferred_element_type=F32)


def dot_nt(a, b):
    return lax.dot_general(a, b, (((1,), (1,)), ((), ())), preferred_element_type=F32)


def dot_tn(a, b):
    return lax.dot_general(a, b, (((0,), (0,)), ((), ())), preferred_element_type=F32)


def kernel(
    z_,
    planes_hbm, cot_hbm, hist_h, stem_kh, stem_gh, stem_sh, first_kh, first_gh, first_sh, second_kh, second_gh, second_sh,
    act_hbm, pgrad_hbm, packed,
    hist, stem_k, stem_g, stem_s, first_k, first_g, first_s, second_k, second_g, second_s,
    planes_v, cot_v, act_v, pgrad_v, y_f, vm, e_mat, s_in, s_t, k0, k0f, wtx, w1, w2, wt1, wt2,
    x0, x1, xp, h0, h1, h2, sl0, sl1, g2, big, pre_t, tmp,
    sbuf, kbuf1, kbuf2, ar_a,
    dk1, dk2, rc1, rc2, rx1, rx2, ry1, ry2, rz1, rz2, rw1, rw2,
    dk0, rw0,
    loc, sm_s, sm_r, kg_s, kg_r, ar_s, ar_r, rs_s, rs_r,
):
    n, outer, c_all = z_.n, z_.outer, z_.channels
    block, live, rows, deep = z_.block, z_.live, z_.rows, z_.deep
    board, pos, planes = z_.board, z_.pos, z_.planes
    me = lax.axis_index("dev")
    zi = me // GROUP
    ii = me % GROUP
    qi = ii // 2
    ci = ii % 2

    def dev(o, i):
        return o * GROUP + i

    def remote(src, dst, send, recv, target):
        copy = pltpu.make_async_remote_copy(
            src_ref=src, dst_ref=dst, send_sem=send, recv_sem=recv, device_id=(target,), device_id_type=MESH
        )
        copy.start()

    bits = n.bit_length() - 1
    steps = [(1 - 2 * (me // 2**b % 2)) * 2**b for b in range(bits)]

    def everyone(visit):
        for p in range(n - 1, 0, -1):
            visit(me + sum(steps[b] for b in range(bits) if p // 2**b % 2))

    outer_peers = [lax.rem(zi + k, outer) for k in range(1, outer)]
    inner_peers = [lax.rem(ii + k, GROUP) for k in range(1, GROUP)]
    quad_peers = [lax.rem(qi + k, QUAD) for k in range(1, QUAD)]
    sibling = dev(zi, qi * 2 + (1 - ci))

    loads = []
    for k, (src, dst) in enumerate((
        (stem_kh, stem_k), (stem_gh, stem_g), (stem_sh, stem_s), (first_kh, first_k), (first_gh, first_g),
        (first_sh, first_s), (second_kh, second_k), (second_gh, second_g), (second_sh, second_s), (hist_h, hist),
    )):
        copy = pltpu.make_async_copy(src, dst, loc.at[4 + k])
        copy.start()
        loads.append(copy)
    load_planes = pltpu.make_async_copy(planes_hbm, planes_v, loc.at[0])
    load_planes.start()
    load_cot = pltpu.make_async_copy(cot_hbm, cot_v, loc.at[1])
    load_cot.start()
    barrier = pltpu.get_barrier_semaphore()

    def greet(other):
        pl.semaphore_signal(barrier, inc=1, device_id=(other,), device_id_type=MESH)

    for o in outer_peers:
        greet(dev(o, ii))
    for i in inner_peers:
        greet(dev(zi, i))
    for copy in loads:
        copy.wait()
    lane = iota((16, 128), 1)
    row = iota((16, 128), 0)

    def placed(vec_ref, slot):
        tmp[0:8, :] = jnp.zeros((8, 128), F32)
        tmp[0:1, 0 : z_.vec] = vec_ref[...].astype(F32)
        start = me * z_.vec
        spread = pltpu.roll(tmp[0:8, :], lax.rem(start, 128), 1)[0:1, :]
        return jnp.where(row == slot + start // 128, spread, 0.0)

    length = z_.stem_len
    off = lax.rem(me * length, c_all)
    tmp[0:16, :] = jnp.zeros((16, 128), F32)
    for r in range(length // 128):
        tmp[r : r + 1, :] = stem_k[pl.ds(128 * r, 128)].astype(F32).reshape(1, 128)
    rest = length % 128
    if rest:
        r = length // 128
        tmp[r : r + 1, 0:rest] = stem_k[pl.ds(128 * r, rest)].astype(F32).reshape(1, rest)
    shift = lax.rem(off, 128)
    rolled = pltpu.roll(tmp[0:16, :], shift, 1)
    flat = jnp.where(lane >= shift, rolled, pltpu.roll(rolled, 1, 0))
    flat = jnp.where(off // 128 == 1, pltpu.roll(flat, 1, 0), flat)
    tmp[0:16, :] = flat
    left = tmp[pl.ds(0, 8, stride=2), :]
    right = tmp[pl.ds(1, 8, stride=2), :]
    vectors = placed(stem_g, 12) + placed(stem_s, 14)
    tmp[0:16, :] = vectors
    tmp[0:6, :] = left[0:6, :]
    tmp[6:12, :] = right[0:6, :]
    sbuf[zi, ii] = tmp[0:16, :].astype(BF16)

    kr = z_.krows

    def kernel_message(k_ref, g_ref, s_ref, buf):
        vectors = placed(g_ref, 0) + placed(s_ref, 2)
        tmp[0 : 2 * kr, :] = k_ref[...].astype(F32)
        left = tmp[pl.ds(0, kr, stride=2), :]
        right = tmp[pl.ds(1, kr, stride=2), :]
        tmp[0:kr, :] = left
        tmp[kr : 2 * kr, :] = right
        tmp[2 * kr : 2 * kr + 16, :] = vectors
        buf[zi, qi, ci] = tmp[0 : z_.kmsg, :].astype(BF16)

    kernel_message(first_k, first_g, first_s, kbuf1)

    def gather_near(g, block_o, o):
        for q in quad_peers:
            remote(block_o, block_o, kg_s.at[g, 1], kg_r.at[g, 1, o], dev(zi, q * 2 + ci))

    def gather_begin(g, buf):
        mine = buf.at[zi, qi, ci]
        for o in outer_peers:
            remote(mine, mine, kg_s.at[g, 0], kg_r.at[g, 0, zi], dev(o, ii))
        gather_near(g, mine, zi)

    def gather_quad(g, buf):
        for o in outer_peers:
            block_o = buf.at[o, qi, ci]
            wait_bytes(block_o, kg_r.at[g, 0, o])
            gather_near(g, block_o, o)

    def gather_core(g, buf, which):
        for o in which:
            wait_bytes(buf.at[o, pl.ds(0, QUAD - 1), 0], kg_r.at[g, 1, o])
            remote(buf.at[o, :, ci], buf.at[o, :, ci], kg_s.at[g, 2], kg_r.at[g, 2, o], sibling)

    def gather_end(g, buf, w):
        many = 16 // math.gcd(16, kr)

        def place(p, vectors):
            there = w.at[pl.ds(pl.multiple_of(p * many * kr, 16), many * kr)]
            for d in range(many):
                s = p * many + d
                piece = buf.at[s // GROUP, (s % GROUP) // 2, s % 2]
                there[kr * d : kr * d + kr, 0:128] = piece[0:kr, :]
                there[kr * d : kr * d + kr, 128:256] = piece[kr : 2 * kr, :]
                vectors += piece[2 * kr : z_.kmsg, :].astype(F32)[0:4, :]
            return vectors

        vectors = jnp.zeros((4, 128), F32)
        for o in [zi] + outer_peers:
            wait_bytes(buf.at[o, :, 0], kg_r.at[g, 2, o])
            each = GROUP // many
            for p in range(each):
                vectors = place(o * each + p, vectors)
        return wide(vectors[0:2, :]), wide(vectors[2:4, :])

    def wide(two_rows):
        return jnp.concatenate([two_rows[0:1, :], two_rows[1:2, :]], axis=1)

    pl.semaphore_wait(barrier, outer - 1 + GROUP - 1)
    for o in outer_peers:
        remote(sbuf.at[zi, ii], sbuf.at[zi, ii], sm_s.at[0], sm_r.at[0], dev(o, ii))
    gather_begin(0, kbuf1)

    load_planes.wait()
    for i in range(board):
        y_f[i * 128 : i * 128 + 128, :] = jnp.zeros((128, 128), F32)
        for k in range(planes):
            y_f[i * 128 + pos * k : i * 128 + pos * k + pos, 0:board] = planes_v[i, k].astype(F32)
    rep = (iota((block, 128), 0) // pos == iota((block, 128), 1)).astype(BF16)
    tmp[0:8, :] = jnp.zeros((8, 128), F32)
    tmp[0:pos, 0:8] = hist[...].astype(F32)
    spread = (iota((128, 128), 1) // (2 * pos) == iota((128, 128), 0)).astype(BF16)
    present = dot(tmp[0:8, :].astype(BF16), spread)
    lane8 = iota((8, 128), 1)
    present = jnp.where(lane8 // pos == planes - 1, 1.0, present)
    present = jnp.sum(jnp.where((lane8 % pos == iota((8, 128), 0)) & (lane8 < planes * pos), present, 0.0), axis=0, keepdims=True)
    lane_b = iota((block, 128), 1)
    pick = jnp.where(lane_b % pos == iota((block, 128), 0) % pos, present, 0.0)
    wider = (iota((128, 128), 1) // pos == iota((128, 128), 0)).astype(BF16)
    for m in range(0, board, 5):
        count = min(5, board - m)
        spread_t = dot(y_f[m * 128 : (m + count) * 128, :].astype(BF16), wider)
        for i in range(count):
            v = jnp.transpose(spread_t[i * 128 : i * 128 + 128, :])[0:block, :] * pick
            at = slice((m + i + 1) * block, (m + i + 2) * block)
            vm[0, at, :] = pltpu.roll(v, pos, 0).astype(BF16)
            vm[1, at, :] = v.astype(BF16)
            vm[2, at, :] = pltpu.roll(v, block - pos, 0).astype(BF16)

    wait_bytes(sbuf.at[pl.ds(0, outer - 1), 0], sm_r.at[0])
    for i in inner_peers:
        remote(sbuf.at[:, ii], sbuf.at[:, ii], sm_s.at[1], sm_r.at[1], dev(zi, i))
    gather_quad(0, kbuf1)
    kernel_message(second_k, second_g, second_s, kbuf2)
    gather_begin(1, kbuf2)

    for b in range(3):
        vm[b, 0:block, :] = jnp.zeros((block, 128), BF16)
        vm[b, block + rows :, :] = jnp.zeros((z_.tall - block - rows, 128), BF16)
    for t in range(9):
        er = iota((128, z_.width), 0)
        e_mat[128 * t : 128 * t + 128, :] = (
            (iota((128, z_.width), 1) == planes * t + er // pos) & (er < planes * pos)
        ).astype(BF16)

    cuts = [0] + [min(m, board) for m in range(3, board, 6)] + [board]
    tiles = [(m, end - m) for m, end in zip(cuts, cuts[1:])]

    def taps(x, start, count):
        return jnp.concatenate([x[t % 3, start + (t // 3) * block : start + (t // 3) * block + count, :] for t in range(9)], axis=1)

    for m, count in tiles:
        s_in[m * block : (m + count) * block, :] = dot(taps(vm, m * block, count * block), e_mat[...]).astype(BF16)
    gather_core(0, kbuf1, [zi])

    k0f[...] = jnp.zeros(k0f.shape, F32)

    for x in (x0, x1, xp):
        for b in range(3):
            x[b, 0:block, :] = jnp.zeros((block, c_all), BF16)
            x[b, block + rows :, :] = jnp.zeros((z_.tall - block - rows, c_all), BF16)

    wait_bytes(sbuf.at[:, pl.ds(0, GROUP - 1)], sm_r.at[1])
    vectors = jnp.zeros((4, 128), F32)
    for s in range(n):
        piece = sbuf[s // GROUP, s % GROUP].astype(F32)
        base = s * length // c_all
        apart = s % 2 if z_.stem_apart else 0
        if z_.stem_apart:
            k0f[apart, base : base + 6, 0:128] = piece[0:6, :]
            k0f[apart, base : base + 6, 128:256] = piece[6:12, :]
        else:
            k0f[0, base : base + 6, 0:128] += piece[0:6, :]
            k0f[0, base : base + 6, 128:256] += piece[6:12, :]
        vectors += piece[12:16, :]
    gain0, shift0 = wide(vectors[0:2, :]), wide(vectors[2:4, :])
    k0[...] = jnp.zeros(k0.shape, BF16)
    used = up(9 * planes, 16)
    k0[0:used, :] = (k0f[0, 0:used, :] + k0f[1, 0:used, :]).astype(BF16)

    blk_mask = iota((block, c_all), 0) < live

    def fold(v):
        return jnp.sum(v.reshape(block // 8, 8, c_all), axis=0)

    def part(i, ahead=0):
        return slice((i + ahead) * block, (i + ahead + 1) * block)

    class Sums:
        def __init__(self):
            self.a = self.b = None

        def add(self, a, b):
            a, b = fold(a), fold(b)
            self.a = a if self.a is None else self.a + a
            self.b = b if self.b is None else self.b + b

        def rows(self):
            return jnp.sum(self.a, axis=0, keepdims=True), jnp.sum(self.b, axis=0, keepdims=True)

    def phase(x, w, produce, consume, between=None, before=None, whole=False):
        done = 0
        if before is not None:
            for i in range(board):
                produce(i)
            done = board
            before()
        for k, (m, count) in enumerate(tiles):
            upto = min(board, m + count + 1)
            for i in range(done, upto):
                produce(i)
            done = max(done, upto)
            out = dot(taps(x, m * block, count * block), w[...])
            if k + 1 < len(tiles):
                upto = min(board, tiles[k + 1][0] + tiles[k + 1][1] + 1)
                for i in range(done, upto):
                    produce(i)
                done = max(done, upto)
            if whole:
                consume(m, count, out)
            else:
                for i in range(count):
                    consume(m + i, out[i * block : (i + 1) * block, :])
            if between is not None:
                between(k)

    def reduce_begin(k, a, b):
        mine = ar_a.at[k, me]
        mine[0:1, :] = a[:, 0:128]
        mine[1:2, :] = a[:, 128:256]
        mine[2:3, :] = b[:, 0:128]
        mine[3:4, :] = b[:, 128:256]

        everyone(lambda other: remote(mine, mine, ar_s.at[k], ar_r.at[k], other))

    def reduce_end(k):
        wait_bytes(ar_a.at[k, pl.ds(0, n - 1)], ar_r.at[k])
        total = jnp.sum(ar_a[k], axis=0)
        return wide(total[0:2, :]), wide(total[2:4, :])

    def bn(total, squares, gain, shift):
        centre = total * (1.0 / z_.cells)
        variance = squares * (1.0 / z_.cells) - centre * centre
        inv = lax.rsqrt(variance + EPSILON)
        scale = gain * inv
        return inv, -centre * inv, scale, shift - centre * scale

    def put(x, i, v):
        at = part(i, 1)
        x[0, at, :] = pltpu.roll(v, pos, 0).astype(BF16)
        x[1, at, :] = v.astype(BF16)
        x[2, at, :] = pltpu.roll(v, block - pos, 0).astype(BF16)

    def activation(h, x, slope, stats):
        _, _, scale, bias = stats

        def produce(i):
            v = h[part(i), :] * scale + bias
            sig = 0.5 * jnp.tanh(0.5 * v) + 0.5
            act = v * sig
            slope[part(i), :] = jnp.where(blk_mask, sig + act * (1.0 - sig), 0.0)
            put(x, i, jnp.where(blk_mask, act, 0.0))

        return produce

    def keep_moments(h, total):
        def consume(i, out):
            h[part(i), :] = out
            v = jnp.where(blk_mask, out, 0.0)
            total.add(v, v * v)

        return consume

    def pre_gradient(g, h, stats, shift_grad, gain_grad, flip=True):
        inv, neg, scale, _ = stats
        a = shift_grad * (1.0 / z_.cells)
        b = gain_grad * (1.0 / z_.cells)
        flipped = [0]

        def produce(i):
            normed = h[part(i), :] * inv + neg
            v = scale * (g[part(i), :] - a - normed * b)
            put(xp, i, jnp.where(blk_mask, v, 0.0))
            if not flip:
                return
            upto = (i + 1) * block // 128 if i + 1 < board else deep // 128
            for k in range(flipped[0], upto):
                pre_t[:, 128 * k : 128 * k + 128] = jnp.transpose(xp[1, block + 128 * k : block + 128 * k + 128, :])
            flipped[0] = upto

        return produce

    def kernel_grad(x, dk, after):
        for t in range(9):
            o = dot(pre_t[...], x[t % 3, (t // 3) * block : (t // 3) * block + deep, :])
            o = jnp.transpose(o)
            r = 256 * t
            while r < 256 * t + 256:
                s, inner = r // kr, r % kr
                count = min(kr - inner, 256 * t + 256 - r)
                rows_o = o[r - 256 * t : r - 256 * t + count, :].astype(BF16)
                here = dk.at[s // GROUP, (s % GROUP) // 2, s % 2]
                here[inner : inner + count, :] = rows_o[:, 0:128]
                here[kr + inner : kr + inner + count, :] = rows_o[:, 128:256]
                r += count
            after(t)

    def transpose_weights(w, wt):
        for t in range(9):
            wt[256 * t : 256 * t + 256, :] = jnp.transpose(w[256 * (8 - t) : 256 * (8 - t) + 256, :])

    def scatter_core(k, dk, rc, which):
        for o in which:
            remote(dk.at[o, :, 1 - ci], rc.at[o], rs_s.at[k, 0], rs_r.at[k, 0, o], sibling)

    def scatter_quad(k, dk, rc, rx, ry, which):
        for o in which:
            wait_bytes(rc.at[o], rs_r.at[k, 0, o])
            for q in range(QUAD):
                rx[o, q] = (dk[o, q, ci].astype(F32) + rc[o, q].astype(F32)).astype(BF16)
            for q in quad_peers:
                remote(rx.at[o, q], ry.at[o, qi], rs_s.at[k, 1], rs_r.at[k, 1, o], dev(zi, q * 2 + ci))

    def scatter_begin(k, dk, rc, rx, ry):
        def complete(t):
            return range(256 * t // (GROUP * kr), 256 * (t + 1) // (GROUP * kr)) if t >= 0 else ()

        def after(t):
            scatter_core(k, dk, rc, complete(t))
            scatter_quad(k, dk, rc, rx, ry, complete(t - 2))
            if t == 8:
                scatter_quad(k, dk, rc, rx, ry, complete(7))
                scatter_quad(k, dk, rc, rx, ry, complete(8))

        return after

    def scatter_outer(k, rx, ry, rz, rw):
        for o in outer_peers + [zi]:
            wait_bytes(ry.at[o, pl.ds(0, QUAD - 1)], rs_r.at[k, 1, o])
            ry[o, qi] = rx[o, qi]
            v = ry[o, 0].astype(F32)
            for q in range(1, QUAD):
                v = v + ry[o, q].astype(F32)
            rz[o] = v.astype(BF16)
            if o is not zi:
                remote(rz.at[o], rw.at[zi], rs_s.at[k, 2], rs_r.at[k, 2, 0], dev(o, ii))

    def scatter_end(k, rz, rw):
        wait_bytes(rw.at[pl.ds(0, outer - 1)], rs_r.at[k, 2, 0])
        rw[zi] = rz[zi]
        v = rw[0].astype(F32)
        for o in range(1, outer):
            v = v + rw[o].astype(F32)
        return v

    def my_part(vector, out):
        start = me * z_.vec
        half = jnp.where(start // 128 == 0, vector[:, 0:128], vector[:, 128:256])
        half = jnp.broadcast_to(half, (8, 128))
        packed[out : out + 1, :] = pltpu.roll(half, lax.rem(128 - lax.rem(start, 128), 128), 1)[0:1, :]

    if z_.gmsg > 2 * kr:
        for dk in (dk1, dk2):
            for s in range(n):
                dk[s // GROUP, (s % GROUP) // 2, s % 2, 2 * kr :, :] = jnp.zeros((z_.gmsg - 2 * kr, 128), BF16)

    total = Sums()
    keep = keep_moments(h0, total)
    for m, count in tiles:
        out = dot(s_in[m * block : (m + count) * block, :], k0[...])
        for i in range(count):
            keep(m + i, out[i * block : (i + 1) * block, :])
    reduce_begin(0, *total.rows())
    gather_quad(1, kbuf2)
    load_cot.wait()
    g2[...] = jnp.zeros(g2.shape, F32)

    def unpack_cot(i, carry):
        here = g2.at[pl.ds(pl.multiple_of(i * block, block), block)]
        for j in range(board):
            here[pos * j : pos * j + pos, :] = cot_v[i, j].astype(F32)
        return carry

    lax.fori_loop(0, board, unpack_cot, 0)
    gather_core(0, kbuf1, outer_peers)
    gather_core(1, kbuf2, [zi])
    stats0 = bn(*reduce_end(0), gain0, shift0)

    total = Sums()
    affine1 = []
    phase(
        x0, w1, activation(h0, x0, sl0, stats0), keep_moments(h1, total),
        before=lambda: affine1.extend(gather_end(0, kbuf1, w1)),
    )
    reduce_begin(1, *total.rows())
    gather_core(1, kbuf2, outer_peers)
    k0t = jnp.transpose(k0[...])
    for t in range(9):
        mr = iota((z_.width, 128), 0)
        ml = iota((z_.width, 128), 1)
        sel = ((mr == planes * (8 - t) + ml // pos) & (ml < planes * pos)).astype(BF16)
        wtx[256 * t : 256 * t + 256, :] = dot(k0t, sel).astype(BF16)
    s_in[rows:deep, :] = jnp.zeros((deep - rows, z_.width), BF16)
    for k in range(deep // 128):
        s_t[:, 128 * k : 128 * k + 128] = jnp.transpose(s_in[128 * k : 128 * k + 128, :])
    gain2, shift2 = gather_end(1, kbuf2, w2)
    stats1 = bn(*reduce_end(1), *affine1)

    total = Sums()
    phase(x1, w2, activation(h1, x1, sl1, stats1), keep_moments(h2, total))
    reduce_begin(2, *total.rows())
    transpose_weights(w2, wt2)
    stats2 = bn(*reduce_end(2), gain2, shift2)

    total = Sums()
    inv, neg, scale, bias = stats2
    for i in range(board):
        at = part(i)
        h = h2[at, :]
        summed = h * scale + bias + x0[1, part(i, 1), :].astype(F32)
        sig = 0.5 * jnp.tanh(0.5 * summed) + 0.5
        act = summed * sig
        big[at, :] = act
        g = g2[at, :] * (sig + act * (1.0 - sig))
        g2[at, :] = g
        total.add(g, g * (h * inv + neg))
    reduce_begin(3, *total.rows())

    def pack_act(i, carry):
        v = big[pl.ds(pl.multiple_of(i * block, block), block), :]
        for j in range(board):
            act_v[i, j] = v[pos * j : pos * j + pos, :].astype(BF16)
        return carry

    lax.fori_loop(0, board, pack_act, 0)
    store_act = pltpu.make_async_copy(act_v, act_hbm, loc.at[2])
    store_act.start()
    transpose_weights(w1, wt1)
    shift_grad, gain_grad = reduce_end(3)

    total1 = Sums()

    def first_consume(i, out):
        inv, neg, _, _ = stats1
        g = out * sl1[part(i), :]
        big[part(i), :] = g
        total1.add(g, g * (h1[part(i), :] * inv + neg))

    phase(xp, wt2, pre_gradient(g2, h2, stats2, shift_grad, gain_grad), first_consume)
    reduce_begin(4, *total1.rows())
    my_part(shift_grad, z_.vec_row + 5)
    my_part(gain_grad, z_.vec_row + 4)
    kernel_grad(x1, dk2, scatter_begin(2, dk2, rc2, rx2, ry2))
    shift_grad, gain_grad = reduce_end(4)

    total0 = Sums()

    def stem_consume(i, out):
        inv, neg, _, _ = stats0
        g = (out + g2[part(i), :]) * sl0[part(i), :]
        big[part(i), :] = g
        total0.add(g, g * (h0[part(i), :] * inv + neg))

    phase(xp, wt1, pre_gradient(big, h1, stats1, shift_grad, gain_grad), stem_consume)
    reduce_begin(5, *total0.rows())
    my_part(shift_grad, z_.vec_row + 3)
    my_part(gain_grad, z_.vec_row + 2)
    kernel_grad(x0, dk1, scatter_begin(1, dk1, rc1, rx1, ry1))
    scatter_outer(2, rx2, ry2, rz2, rw2)
    shift_grad, gain_grad = reduce_end(5)

    rep_rows = jnp.concatenate([rep, jnp.zeros((128 - block, 128), BF16)], axis=0)
    rep_twice = jnp.concatenate([rep_rows, rep_rows], axis=0)
    gap = jnp.zeros((128 - block, 128), F32)

    def planes_consume(m, count, out):
        flat = []
        for i in range(count):
            v = jnp.transpose(jnp.concatenate([out[i * block : (i + 1) * block, :] * pick, gap], axis=0))
            hi = v.astype(BF16)
            flat.append(jnp.concatenate([hi, (v - hi.astype(F32)).astype(BF16)], axis=1))
        w = dot(jnp.concatenate(flat, axis=0), rep_twice)
        for i in range(count):
            for k in range(planes):
                pgrad_v[m + i, k] = w[128 * i + pos * k : 128 * i + pos * k + pos, 0:board]
        store = pltpu.make_async_copy(pgrad_v.at[pl.ds(m, count)], pgrad_hbm.at[pl.ds(m, count)], loc.at[14 + len(stores)])
        store.start()
        stores.append(store)

    stores = []

    def stem_before():
        big[0 : z_.width, :] = dot(s_t[...], xp[1, block : block + deep, :])
        for s in range(n):
            base = s * length // c_all
            dk0[s, 0:6, :] = big[base : base + 6, 0:128].astype(BF16)
            dk0[s, 6:12, :] = big[base : base + 6, 128:256].astype(BF16)
            dk0[s, 12:16, :] = jnp.zeros((4, 128), BF16)

        everyone(lambda other: remote(dk0.at[other], rw0.at[me], rs_s.at[0, 0], rs_r.at[0, 0, 0], other))

    def stem_between(k):
        if k == 1:
            scatter_outer(1, rx1, ry1, rz1, rw1)

    phase(xp, wtx, pre_gradient(big, h0, stats0, shift_grad, gain_grad, False), planes_consume, stem_between, stem_before, True)
    my_part(shift_grad, z_.vec_row + 1)
    my_part(gain_grad, z_.vec_row + 0)

    def spill(v, out):
        tmp[0 : 2 * kr, :] = v[0 : 2 * kr, :]
        packed[pl.ds(out, kr, stride=2), :] = tmp[0:kr, :]
        packed[pl.ds(out + 1, kr, stride=2), :] = tmp[kr : 2 * kr, :]

    spill(scatter_end(2, rz2, rw2), 0)
    wait_bytes(rw0.at[pl.ds(0, n - 1)], rs_r.at[0, 0, 0])
    rw0[me] = dk0[me]
    v = jnp.sum(rw0[...].astype(F32), axis=0)
    tmp[0:32, :] = jnp.zeros((32, 128), F32)
    tmp[16:32, :] = v
    left = tmp[16:22, :]
    right = tmp[22:28, :]
    tmp[pl.ds(0, 6, stride=2), :] = left
    tmp[pl.ds(1, 6, stride=2), :] = right
    flat = tmp[0:16, :]
    flat = jnp.where(off // 128 == 1, pltpu.roll(flat, 15, 0), flat)
    rolled = pltpu.roll(flat, lax.rem(128 - shift, 128), 1)
    flat = jnp.where(lane < 128 - shift, rolled, pltpu.roll(rolled, 15, 0))
    packed[z_.stem_row : z_.stem_row + 16, :] = flat
    spill(scatter_end(1, rz1, rw1), z_.first_row)

    wait_bytes(sbuf.at[pl.ds(0, outer - 1), 0], sm_s.at[0])
    wait_bytes(sbuf.at[:, pl.ds(0, GROUP - 1)], sm_s.at[1])
    for g, buf in ((0, kbuf1), (1, kbuf2)):
        wait_bytes(buf.at[pl.ds(0, outer - 1), 0, 0], kg_s.at[g, 0])
        wait_bytes(buf.at[:, pl.ds(0, QUAD - 1), 0], kg_s.at[g, 1])
        wait_bytes(buf.at[:, :, 0], kg_s.at[g, 2])
    for k in range(6):
        wait_bytes(ar_a.at[k, pl.ds(0, n - 1)], ar_s.at[k])
    wait_bytes(rw0.at[pl.ds(0, n - 1)], rs_s.at[0, 0])
    for k, rc, ry, rw in ((1, rc1, ry1, rw1), (2, rc2, ry2, rw2)):
        wait_bytes(rc, rs_s.at[k, 0])
        wait_bytes(ry.at[:, pl.ds(0, QUAD - 1)], rs_s.at[k, 1])
        wait_bytes(rw.at[pl.ds(0, outer - 1)], rs_s.at[k, 2])
    store_act.wait()
    for store in stores:
        store.wait()


def unpack_outputs(
    z_, act_in, pgrad_in, packed,
    act, pgrad, stem_kg, stem_gg, stem_sg, first_kg, first_gg, first_sg, second_kg, second_gg, second_sg, sems,
):
    copies = []
    for m in range(0, z_.board, 5):
        rows = pl.ds(m, min(5, z_.board - m))
        for src, dst in ((act_in, act), (pgrad_in, pgrad)):
            copies.append(pltpu.make_async_copy(src.at[rows], dst.at[rows], sems.at[len(copies)]))
    for copy in copies:
        copy.start()
    kr = z_.krows
    second_kg[...] = packed[0 : 2 * kr, :]
    first_kg[...] = packed[z_.first_row : z_.first_row + 2 * kr, :]
    for k, ref in enumerate((stem_gg, stem_sg, first_gg, first_sg, second_gg, second_sg)):
        ref[...] = packed[z_.vec_row + k : z_.vec_row + k + 1, 0 : z_.vec]
    flat = packed[z_.stem_row : z_.stem_row + 16, :]
    length = z_.stem_len
    for r in range(length // 128):
        stem_kg[pl.ds(128 * r, 128)] = flat[r : r + 1, :].reshape(128)
    rest = length % 128
    if rest:
        r = length // 128
        stem_kg[pl.ds(128 * r, rest)] = flat[r : r + 1, 0:rest].reshape(rest)
    for copy in copies:
        copy.wait()


def body(
    planes, history, stem_kernel, stem_gain, stem_shift, first_kernel, first_gain, first_shift,
    second_kernel, second_gain, second_shift, cotangent,
):
    n = lax.axis_size("dev")
    pt = planes.transpose(1, 3, 0, 2)
    ct = cotangent.transpose(1, 2, 0, 3)
    z_ = Sizes(n, pt.shape, ct.shape, stem_kernel.shape[0], first_kernel.shape[0])
    c, o = z_.channels, z_.outer
    lanes_k = first_kernel.shape[0] // 128

    def vm(shape, kind=F32):
        return pltpu.VMEM(shape, kind)

    def out(shape, kind=F32):
        return jax.ShapeDtypeStruct(shape, kind)

    hbm = pl.BlockSpec(memory_space=pl.ANY)
    far = pl.BlockSpec(memory_space=pltpu.HBM)
    near = pl.BlockSpec(memory_space=pltpu.VMEM)
    vec = (1, z_.vec)
    wide = (o, QUAD, 2, z_.gmsg, 128)
    scratch = [
        vm(history.shape, jnp.int32), vm(stem_kernel.shape, BF16), vm(vec, BF16), vm(vec, BF16),
        vm((lanes_k, 128), BF16), vm(vec, BF16), vm(vec, BF16), vm((lanes_k, 128), BF16), vm(vec, BF16), vm(vec, BF16),
        vm(pt.shape, BF16), vm(ct.shape, BF16), vm(ct.shape, BF16), vm(pt.shape),
        vm((z_.board * 128, 128)), vm((3, z_.tall, 128), BF16), vm((9 * 128, z_.width), BF16),
        vm((z_.deep, z_.width), BF16), vm((z_.width, z_.deep), BF16),
        vm((z_.width, c), BF16), vm((2, z_.stem_all, c)), vm((9 * c, 128), BF16),
        vm((9 * c, c), BF16), vm((9 * c, c), BF16), vm((9 * c, c), BF16), vm((9 * c, c), BF16),
        vm((3, z_.tall, c), BF16), vm((3, z_.tall, c), BF16), vm((3, z_.tall, c), BF16),
        vm((z_.rows, c)), vm((z_.rows, c)), vm((z_.rows, c)), vm((z_.rows, c)), vm((z_.rows, c)),
        vm((z_.rows, c)), vm((z_.rows, c)), vm((c, z_.deep), BF16), vm((up(2 * z_.krows + 32, 16), 128)),
        vm((o, GROUP, 16, 128), BF16), vm((o, QUAD, 2, z_.kmsg, 128), BF16), vm((o, QUAD, 2, z_.kmsg, 128), BF16),
        vm((6, n, 4, 128)),
        vm(wide, BF16), vm(wide, BF16), vm((o, QUAD, z_.gmsg, 128), BF16), vm((o, QUAD, z_.gmsg, 128), BF16),
        vm((o, QUAD, z_.gmsg, 128), BF16), vm((o, QUAD, z_.gmsg, 128), BF16),
        vm((o, QUAD, z_.gmsg, 128), BF16), vm((o, QUAD, z_.gmsg, 128), BF16),
        vm((o, z_.gmsg, 128), BF16), vm((o, z_.gmsg, 128), BF16), vm((o, z_.gmsg, 128), BF16), vm((o, z_.gmsg, 128), BF16),
        vm((n, 16, 128), BF16), vm((n, 16, 128), BF16),
        pltpu.SemaphoreType.DMA((14 + up(z_.board, 5) // 5,)), pltpu.SemaphoreType.DMA((2,)), pltpu.SemaphoreType.DMA((2,)),
        pltpu.SemaphoreType.DMA((2, 3)), pltpu.SemaphoreType.DMA((2, 3, o)),
        pltpu.SemaphoreType.DMA((6,)), pltpu.SemaphoreType.DMA((6,)),
        pltpu.SemaphoreType.DMA((3, 3)), pltpu.SemaphoreType.DMA((3, 3, o)),
    ]
    outs = pl.pallas_call(
        functools.partial(kernel, z_),
        out_shape=(out(ct.shape, BF16), out(pt.shape), out((z_.packed, 128))),
        in_specs=[far] * 12,
        out_specs=(hbm, hbm, near),
        scratch_shapes=scratch,
        compiler_params=pltpu.CompilerParams(
            collective_id=0, has_side_effects=True, vmem_limit_bytes=52 * 2**20
        ),
    )(*[
        pltpu.with_memory_space_constraint(v, pltpu.HBM)
        for v in (
            pt, ct, history, stem_kernel, stem_gain.reshape(vec), stem_shift.reshape(vec),
            first_kernel.reshape(lanes_k, 128), first_gain.reshape(vec), first_shift.reshape(vec),
            second_kernel.reshape(lanes_k, 128), second_gain.reshape(vec), second_shift.reshape(vec),
        )
    ])
    outs = pl.pallas_call(
        functools.partial(unpack_outputs, z_),
        out_shape=(
            out(ct.shape, BF16), out(pt.shape), out(stem_kernel.shape), out(vec), out(vec),
            out((lanes_k, 128)), out(vec), out(vec), out((lanes_k, 128)), out(vec), out(vec),
        ),
        in_specs=[hbm, hbm, near],
        out_specs=(hbm, hbm) + (near,) * 9,
        scratch_shapes=[pltpu.SemaphoreType.DMA((2 * up(z_.board, 5) // 5,))],
        compiler_params=pltpu.CompilerParams(vmem_limit_bytes=8 * 2**20),
    )(*outs)
    outs = list(outs)
    outs[0] = outs[0].transpose(2, 0, 1, 3)
    outs[1] = outs[1].transpose(2, 0, 3, 1)
    return tuple(outs[:2]) + tuple(v.reshape(-1) for v in outs[2:])


def solution(mesh):
    split = P("dev")
    return jax.shard_map(
        body, mesh=mesh, in_specs=(split,) * 12, out_specs=(split,) * 11, check_vma=False
    )
```

time: 799 us -> 70.2 us (0.09)
  blocking collectives: 407 us -> 0 us
  waiting for transfers between devices: 206 us -> 0 us
  local copies, waits for them, and re-layouts: 89.2 us -> 0 us
  Pallas kernels: 0 us -> 69.2 us
  other arithmetic: 42.7 us -> 0 us
  matrix products: 31.4 us -> 0 us
  between operations: 15 us -> 0.82 us
    psum x9 -> x0, blocking collectives: 364 us -> none  [the longest x3 123 us: statistics(): centre = lax.psum(jnp.sum(pre_value, axis=(0, 1, 2)), 'dev') / total_cells]
    unnamed x6 -> x0, waiting for transfers between devices: 206 us -> none
    pallas_call x0 -> x2, Pallas kernels: none -> 69.2 us  [the longest x1 67.4 us: body(): pl.pallas_call(functools.partial(kernel, z_), out_shape=(out(ct.shape, BF...]
    unnamed x1 -> x0, blocking collectives: 42.1 us -> none
    mul x14 -> x0, local copies, waits for them, and re-layouts: 32.8 us -> none  [the longest x4 15.5 us: swish_slope(): return sigma * (1.0 + value * (1.0 - sigma))]
    conv_general_dilated x9 -> x0, matrix products: 31.4 us -> none  [the longest x6 22.8 us: project(): lax.conv_general_dilated(source, kernel_all, (1, 1), 'SAME', dimension_nu...]
    unnamed x117 -> x0, local copies, waits for them, and re-layouts: 20.4 us -> none
    convert_element_type x19 -> x0, other arithmetic: 18 us -> none  [the longest x4 8.26 us: layer_back(): pre_grad = (gain_all * stats[1] * (norm_grad - shift_grad / total_cells -...]
  transfers between devices with their start and end apart: 4 -> 0, of which waited for: 2 -> 0; matrix products, arithmetic and copies ran while one was open for 6% -> 0% of each run, Pallas kernels for 0% -> 0%
where the time goes in v1:
time: 70.2 us; the launch traced here: 70 us
  Pallas kernels  69.2 us (99%)
  between operations  0.82 us (1%)
    pallas_call x1, Pallas kernels, body(): pl.pallas_call(functools.partial(kernel, z_), out_shape=(out(ct.shape, BF...  67.4 us
    pallas_call x1, Pallas kernels, body(): pl.pallas_call(functools.partial(unpack_outputs, z_), out_shape=(out(ct.s...  1.83 us

profile of v1, /device:TPU:0, one launch (start us, length us, event | category | flops | bytes accessed | tf_op | source)
XLA Modules:
  0.0 70.0 jit_solution(16972968567449159837)
XLA Ops:
  0.6 67.4 %shard_map.203 = (bf16[19,19,4,256]{3,2,1,0:T(4,128)(2,1)S(1)}, f32[19,17,4,19]{3,2,1,0:T(4,128)S(1)}, f32[312,128]{1,0:T(8,128)S(1)}) custom-call(bf16[19,17,4,19]{3,2,1,0:T(4,128)(2,1)} %bitcast.21, bf16[19,19,4,256]{3,2,1,0:T(4,128)(2,1)} %bitcast.20, s32[4,8]{1,0:T(4,128)} %hist_h.1, bf16[1224]{0:T(1024)(128)(2,1)} %stem_kh.1, bf16[1,8]{1,0:T(2,128)(2,1)} %bitcast.24, ...), custom_call_target="tpu_custom_call" | custom-call | tf_op jit(solution)/shard_map/pallas_call | solution.py:750
  68.0 1.8 %shard_map.204 = (bf16[19,19,4,256]{3,2,1,0:T(4,128)(2,1)}, f32[19,17,4,19]{3,2,1,0:T(4,128)}, f32[1224]{0:T(1024)}, f32[1,8]{1,0:T(1,128)}, f32[1,8]{1,0:T(1,12...) custom-call(bf16[19,19,4,256]{3,2,1,0:T(4,128)(2,1)S(1)} %get-tuple-, ...), custom_call_target="tpu_custom_call" | custom-call | tf_op jit(solution)/shard_map/pallas_call | solution.py:767

commit v2 on v1

--- a/solution.py
+++ b/solution.py
@@ -194,8 +194,8 @@
             wait_bytes(block_o, kg_r.at[g, 0, o])
             gather_near(g, block_o, o)
 
-    def gather_core(g, buf, which):
-        for o in which:
+    def gather_core(g, buf):
+        for o in [zi] + outer_peers:
             wait_bytes(buf.at[o, pl.ds(0, QUAD - 1), 0], kg_r.at[g, 1, o])
             remote(buf.at[o, :, ci], buf.at[o, :, ci], kg_s.at[g, 2], kg_r.at[g, 2, o], sibling)
 
@@ -258,8 +258,6 @@
     for i in inner_peers:
         remote(sbuf.at[:, ii], sbuf.at[:, ii], sm_s.at[1], sm_r.at[1], dev(zi, i))
     gather_quad(0, kbuf1)
-    kernel_message(second_k, second_g, second_s, kbuf2)
-    gather_begin(1, kbuf2)
 
     for b in range(3):
         vm[b, 0:block, :] = jnp.zeros((block, 128), BF16)
@@ -278,7 +276,8 @@
 
     for m, count in tiles:
         s_in[m * block : (m + count) * block, :] = dot(taps(vm, m * block, count * block), e_mat[...]).astype(BF16)
-    gather_core(0, kbuf1, [zi])
+    kernel_message(second_k, second_g, second_s, kbuf2)
+    gather_begin(1, kbuf2)
 
     k0f[...] = jnp.zeros(k0f.shape, F32)
 
@@ -420,12 +419,12 @@
     def kernel_grad(x, dk, after):
         for t in range(9):
             o = dot(pre_t[...], x[t % 3, (t // 3) * block : (t // 3) * block + deep, :])
-            o = jnp.transpose(o)
+            o = jnp.transpose(o.astype(BF16))
             r = 256 * t
             while r < 256 * t + 256:
                 s, inner = r // kr, r % kr
                 count = min(kr - inner, 256 * t + 256 - r)
-                rows_o = o[r - 256 * t : r - 256 * t + count, :].astype(BF16)
+                rows_o = o[r - 256 * t : r - 256 * t + count, :]
                 here = dk.at[s // GROUP, (s % GROUP) // 2, s % 2]
                 here[inner : inner + count, :] = rows_o[:, 0:128]
                 here[kr + inner : kr + inner + count, :] = rows_o[:, 128:256]
@@ -498,7 +497,7 @@
         for i in range(count):
             keep(m + i, out[i * block : (i + 1) * block, :])
     reduce_begin(0, *total.rows())
-    gather_quad(1, kbuf2)
+    gather_core(0, kbuf1)
     load_cot.wait()
     g2[...] = jnp.zeros(g2.shape, F32)
 
@@ -509,18 +508,14 @@
         return carry
 
     lax.fori_loop(0, board, unpack_cot, 0)
-    gather_core(0, kbuf1, outer_peers)
-    gather_core(1, kbuf2, [zi])
+    gather_quad(1, kbuf2)
     stats0 = bn(*reduce_end(0), gain0, shift0)
+    gain1, shift1 = gather_end(0, kbuf1, w1)
 
     total = Sums()
-    affine1 = []
-    phase(
-        x0, w1, activation(h0, x0, sl0, stats0), keep_moments(h1, total),
-        before=lambda: affine1.extend(gather_end(0, kbuf1, w1)),
-    )
+    phase(x0, w1, activation(h0, x0, sl0, stats0), keep_moments(h1, total))
     reduce_begin(1, *total.rows())
-    gather_core(1, kbuf2, outer_peers)
+    gather_core(1, kbuf2)
     k0t = jnp.transpose(k0[...])
     for t in range(9):
         mr = iota((z_.width, 128), 0)
@@ -531,7 +526,7 @@
     for k in range(deep // 128):
         s_t[:, 128 * k : 128 * k + 128] = jnp.transpose(s_in[128 * k : 128 * k + 128, :])
     gain2, shift2 = gather_end(1, kbuf2, w2)
-    stats1 = bn(*reduce_end(1), *affine1)
+    stats1 = bn(*reduce_end(1), gain1, shift1)
 
     total = Sums()
     phase(x1, w2, activation(h1, x1, sl1, stats1), keep_moments(h2, total))
@@ -676,28 +671,35 @@
 
 def unpack_outputs(
     z_, act_in, pgrad_in, packed,
-    act, pgrad, stem_kg, stem_gg, stem_sg, first_kg, first_gg, first_sg, second_kg, second_gg, second_sg, sems,
+    act, pgrad, stem_kg, stem_gg, stem_sg, first_kg, first_gg, first_sg, second_kg, second_gg, second_sg,
+    stem_v, g0, s0, g1, s1, g2, s2, sems,
 ):
     copies = []
+
+    def send(src, dst):
+        copies.append(pltpu.make_async_copy(src, dst, sems.at[len(copies)]))
+        copies[-1].start()
+
     for m in range(0, z_.board, 5):
         rows = pl.ds(m, min(5, z_.board - m))
-        for src, dst in ((act_in, act), (pgrad_in, pgrad)):
-            copies.append(pltpu.make_async_copy(src.at[rows], dst.at[rows], sems.at[len(copies)]))
-    for copy in copies:
-        copy.start()
+        send(act_in.at[rows], act.at[rows])
+        send(pgrad_in.at[rows], pgrad.at[rows])
     kr = z_.krows
-    second_kg[...] = packed[0 : 2 * kr, :]
-    first_kg[...] = packed[z_.first_row : z_.first_row + 2 * kr, :]
-    for k, ref in enumerate((stem_gg, stem_sg, first_gg, first_sg, second_gg, second_sg)):
-        ref[...] = packed[z_.vec_row + k : z_.vec_row + k + 1, 0 : z_.vec]
+    send(packed.at[pl.ds(0, 2 * kr)], second_kg)
+    send(packed.at[pl.ds(z_.first_row, 2 * kr)], first_kg)
     flat = packed[z_.stem_row : z_.stem_row + 16, :]
     length = z_.stem_len
     for r in range(length // 128):
-        stem_kg[pl.ds(128 * r, 128)] = flat[r : r + 1, :].reshape(128)
+        stem_v[pl.ds(128 * r, 128)] = flat[r : r + 1, :].reshape(128)
     rest = length % 128
     if rest:
         r = length // 128
-        stem_kg[pl.ds(128 * r, rest)] = flat[r : r + 1, 0:rest].reshape(rest)
+        stem_v[pl.ds(128 * r, rest)] = flat[r : r + 1, 0:rest].reshape(rest)
+    send(stem_v, stem_kg)
+    pairs = ((g0, stem_gg), (s0, stem_sg), (g1, first_gg), (s1, first_sg), (g2, second_gg), (s2, second_sg))
+    for k, (here, out) in enumerate(pairs):
+        here[...] = packed[z_.vec_row + k : z_.vec_row + k + 1, 0 : z_.vec]
+        send(here, out)
     for copy in copies:
         copy.wait()
 
@@ -771,8 +773,8 @@
             out((lanes_k, 128)), out(vec), out(vec), out((lanes_k, 128)), out(vec), out(vec),
         ),
         in_specs=[hbm, hbm, near],
-        out_specs=(hbm, hbm) + (near,) * 9,
-        scratch_shapes=[pltpu.SemaphoreType.DMA((2 * up(z_.board, 5) // 5,))],
+        out_specs=(hbm,) * 11,
+        scratch_shapes=[vm(stem_kernel.shape)] + [vm(vec)] * 6 + [pltpu.SemaphoreType.DMA((2 * up(z_.board, 5) // 5 + 9,))],
         compiler_params=pltpu.CompilerParams(vmem_limit_bytes=8 * 2**20),
     )(*outs)
     outs = list(outs)

time: 70.2 us -> 69 us (0.983)
  Pallas kernels: 69.2 us -> 68 us
where the time goes in v2:
time: 69 us; the launch traced here: 68.8 us
  Pallas kernels  68 us (99%)
  between operations  0.82 us (1%)
    pallas_call x1, Pallas kernels, body(): pl.pallas_call(functools.partial(kernel, z_), out_shape=(out(ct.shape, BF...  66.7 us

profile of v2, /device:TPU:0, one launch (start us, length us, event | category | flops | bytes accessed | tf_op | source)
XLA Modules:
  0.0 68.8 jit_solution(5956988806781625510)
XLA Ops:
  0.6 66.7 %shard_map.203 = (bf16[19,19,4,256]{3,2,1,0:T(4,128)(2,1)S(1)}, f32[19,17,4,19]{3,2,1,0:T(4,128)S(1)}, f32[312,128]{1,0:T(8,128)S(1)}) custom-call(bf16[19,17,4,19]{3,2,1,0:T(4,128)(2,1)} %bitcast.21, bf16[19,19,4,256]{3,2,1,0:T(4,128)(2,1)} %bitcast.20, s32[4,8]{1,0:T(4,128)} %hist_h.1, bf16[1224]{0:T(1024)(128)(2,1)} %stem_kh.1, bf16[1,8]{1,0:T(2,128)(2,1)} %bitcast.24, ...), custom_call_target="tpu_custom_call" | custom-call | tf_op jit(solution)/shard_map/pallas_call | solution.py:752
  67.4 1.3 %shard_map.204 = (bf16[19,19,4,256]{3,2,1,0:T(4,128)(2,1)}, f32[19,17,4,19]{3,2,1,0:T(4,128)}, f32[1224]{0:T(1024)}, f32[1,8]{1,0:T(1,128)}, f32[1,8]{1,0:T(1,12...) custom-call(bf16[19,19,4,256]{3,2,1,0:T(4,128)(2,1)S(1)} %get-tuple-, ...), custom_call_target="tpu_custom_call" | custom-call | tf_op jit(solution)/shard_map/pallas_call | solution.py:769
